TPU v7x, 32 devices: a whole 2x2x4 slice. The times are simulated.
32 devices in a mesh: row: 8 (over z, y), col: 4 (over x, core).
Axes of the slice: x: 2, y: 2, z: 4, core: 2. Of those that a mesh axis runs over, the one named last changes fastest.
Arguments:
- child_update: bfloat16 [32768, 16384], P('row', 'col'), may hold values from -6 to 6
- child_map: int32 [2, 128], replicated, may hold values from 0 to 191, as said below
- tile_mask: int32 [192, 192], replicated, may hold values 0 or 1
- diag_inverse: bfloat16 [768, 768], replicated, may hold values from -0.0078125 to 0.0078125
Outputs:
- factored: bfloat16 [24576, 24576], P('row', 'col')
Inputs may be any that keep to these rules, and one draw needn't show every extreme that they name: Each row of child_map holds distinct parent blocks. Of each aligned run of 32 entries of a row, at most 4 lie in any one aligned run of 24 parent blocks, and every such run that is hit holds exactly 4; of each aligned run of 32 entries, at most 8 lie in any one aligned run of 48 parent blocks, and every run hit holds exactly 8.
All inputs are finite; a program needn't handle non-finite values.
Results may differ from a plain program's by a relative error of at most 0.0042.
Values may be sent and summed in bfloat16 or wider, within the bound.
A program may use at most 384 MiB of HBM per device.

v0:
```python
import jax
import jax.numpy as jnp
from jax import lax
from jax.sharding import PartitionSpec as P

CB = 128
NPB = 192
PW = 768


def broadcast(x, axis, root):
    mine = lax.axis_index(axis) == root
    return lax.psum(jnp.where(mine, x, jnp.zeros_like(x)), axis)


def slot_table(parents, owner_blocks, dest_count, capacity):
    count = parents.shape[0]
    places = jnp.arange(count, dtype=jnp.int32)
    target = parents // owner_blocks
    same = target[:, None] == target[None, :]
    before = places[None, :] < places[:, None]
    rank = jnp.sum((same & before).astype(jnp.int32), axis=1)
    hits = (target[None, None, :] == jnp.arange(dest_count, dtype=jnp.int32)[:, None, None]) & (
        rank[None, None, :] == jnp.arange(capacity, dtype=jnp.int32)[None, :, None]
    )
    filled = jnp.any(hits, axis=2)
    source = jnp.sum(jnp.where(hits, places[None, None, :], 0), axis=2)
    ident = jnp.where(filled, jnp.sum(jnp.where(hits, parents[None, None, :], 0), axis=2), -1)
    return (source, filled, ident)


def run_slice(values, start, length):
    return lax.dynamic_slice_in_dim(values, start, length, 0)


def body(child_update, child_map, tile_mask, diag_inverse):
    row_count = lax.axis_size("row")
    col_count = lax.axis_size("col")
    per_child = row_count // 2
    row_index = lax.axis_index("row")
    col_index = lax.axis_index("col")
    child = row_index // per_child
    within = row_index % per_child
    row_blocks = child_update.shape[0] // CB
    col_blocks = child_update.shape[1] // CB
    own_rows = NPB // row_count
    own_cols = NPB // col_count
    cap_rows = 2 * (16 // row_count) * max(1, 8 // row_count)
    cap_cols = 128 // (col_count * col_count)
    zero_value = jnp.zeros((), jnp.bfloat16)

    def row_table(child_id, shard):
        return slot_table(
            run_slice(child_map[child_id], shard * row_blocks, row_blocks),
            own_rows,
            row_count,
            cap_rows,
        )

    def col_table(child_id, shard):
        return slot_table(
            run_slice(child_map[child_id], shard * col_blocks, col_blocks),
            own_cols,
            col_count,
            cap_cols,
        )

    row_source, row_filled, _ = row_table(child, within)
    tiles = child_update.reshape(row_blocks, CB, col_blocks, CB)
    by_rows = jnp.take(tiles, row_source.reshape(-1), axis=0).reshape(
        row_count, cap_rows, CB, col_blocks, CB
    )
    by_rows = jnp.where(row_filled[:, :, None, None, None], by_rows, zero_value)
    arrived_rows = lax.all_to_all(by_rows, "row", split_axis=0, concat_axis=0, tiled=True)
    arrived_rows = arrived_rows.reshape(2, per_child, cap_rows, CB, col_blocks, CB)
    stacked = []
    for child_id in range(2):
        col_source, col_filled, _ = col_table(child_id, col_index)
        taken = jnp.take(arrived_rows[child_id], col_source.reshape(-1), axis=3).reshape(
            per_child, cap_rows, CB, col_count, cap_cols, CB
        )
        stacked.append(jnp.where(col_filled[None, None, None, :, :, None], taken, zero_value))
    arrived = lax.all_to_all(jnp.stack(stacked), "col", split_axis=4, concat_axis=4, tiled=True)
    layout = "hsiatj"
    row_shards = jnp.arange(per_child, dtype=jnp.int32)
    col_shards = jnp.arange(col_count, dtype=jnp.int32)
    row_slots = jnp.arange(own_rows, dtype=jnp.int32)
    col_slots = jnp.arange(own_cols, dtype=jnp.int32)
    front_sum = jnp.zeros((own_rows, CB, own_cols, CB), jnp.float32)
    for child_id in range(2):

        def row_ident(shard):
            return row_table(child_id, shard)[2][row_index]

        def col_ident(shard):
            return col_table(child_id, shard)[2][col_index]

        row_ids = jax.vmap(row_ident)(row_shards) - row_index * own_rows
        col_ids = jax.vmap(col_ident)(col_shards) - col_index * own_cols
        row_pick = (row_ids[:, :, None] == row_slots[None, None, :]).astype(jnp.bfloat16)
        col_pick = (col_ids[:, :, None] == col_slots[None, None, :]).astype(jnp.bfloat16)
        placed = jnp.einsum(
            "hsI," + layout + "->Iiatj",
            row_pick,
            arrived[child_id],
            preferred_element_type=jnp.float32,
        ).astype(jnp.bfloat16)
        front_sum = front_sum + jnp.einsum(
            "atJ,Iiatj->IiJj", col_pick, placed, preferred_element_type=jnp.float32
        )
    front = front_sum.reshape(own_rows * CB, own_cols * CB).astype(jnp.bfloat16)
    global_rows = row_index * own_rows * CB + jnp.arange(own_rows * CB, dtype=jnp.int32)[:, None]
    global_cols = col_index * own_cols * CB + jnp.arange(own_cols * CB, dtype=jnp.int32)[None, :]
    lower = jnp.dot(front[:, :PW], diag_inverse, preferred_element_type=jnp.float32)
    lower = jnp.where(global_rows >= PW, lower, jnp.float32(0.0)).astype(jnp.bfloat16)
    lower = broadcast(lower, "col", 0)
    upper = broadcast(front[:PW, :], "row", 0)
    keep = lax.dynamic_slice(
        tile_mask, (row_index * own_rows, col_index * own_cols), (own_rows, own_cols)
    ).astype(jnp.float32)
    update = jnp.dot(lower, upper, preferred_element_type=jnp.float32)
    update = (update.reshape(own_rows, CB, own_cols, CB) * keep[:, None, :, None]).reshape(
        own_rows * CB, own_cols * CB
    )
    schur = (front.astype(jnp.float32) - update).astype(jnp.bfloat16)
    left = jnp.where(global_rows >= PW, jnp.pad(lower, ((0, 0), (0, own_cols * CB - PW))), front)
    return jnp.where(global_cols < PW, left, schur)


def solution(mesh):
    placed = (P("row", "col"), P(), P(), P())
    return jax.shard_map(
        body, mesh=mesh, in_specs=placed, out_specs=P("row", "col"), check_vma=False
    )
```

profile of v0, /device:TPU:24, one launch (start us, length us, event | category | flops | bytes accessed | tf_op | source)
XLA Modules:
  0.0 1991.0 jit_solution(83739206580313152)
XLA Ops:
  6.5 0.9 bitcast_select_fusion.1
  7.4 0.2 convert_reduce_fusion.5
  8.3 23.1 %copy.47 = bf16[512,8,32,128]{3,2,1,0:T(8,128)(2,1)} copy(bf16[512,8,32,128]{3,1,2,0:T(8,128)(2,1)} %bitcast.140) | data formatting | bytes 67108864
  31.4 22.8 %gather_fusion = bf16[32,128,32,128]{3,2,1,0:T(8,128)(2,1)} fusion(bf16[32,128,32,128]{3,2,1,0:T(8,128)(2,1)} %bitcast.134, s32[1024]{0:T(1024)S(1)} %pad_clamp_fusion.2), kind=kCustom, calls=%fused_computation.2 | custom fusion | bytes 67108992 | tf_op jit(solution)/shard_map/jit(_take)/gather | solution.py:70
  54.3 22.7 %fusion.3 = bf16[8,4,128,32,128]{4,2,3,1,0:T(8,128)(2,1)} fusion(bf16[8,4,128,32,128]{4,3,2,1,0:T(8,128)(2,1)} %bitcast.133, pred[8,4]{1,0:T(8,128)(4,1)S(1)} %copy.28, pred[8,4]{1,0:T(8,128)(4,1)S(1)} %copy.27), kind=kLoop, calls=%fused_computation.18 | loop fusion | flops 33554432 | bytes 67108928 | tf_op jit(solution)/shard_map/jit(_where)/select_n | solution.py:73
  77.0 7.2 all-to-all-start
  84.3 0.2 convert_reduce_fusion.6
  84.8 0.2 convert_reduce_fusion.4
  85.6 719.9 %all-to-all-done = bf16[8,4,128,32,128]{4,2,3,1,0:T(8,128)(2,1)} async-done(((bf16[8,4,128,32,128]{4,2,3,1,0:T(8,128)(2,1)}), bf16[8,4,128,32,128]{4,2,3,1,0:T(8,128)(2,1)}, u32[]{:S(2)}, u32[]{:S(2)}) %all-to-all-start) | async-done | bytes 33554464 | tf_op jit(solution)/shard_map/all_to_all | solution.py:74
  805.6 23.5 %fusion.46 = (bf16[4,4,128,32,128]{4,2,3,1,0:T(8,128)(2,1)}, bf16[4,4,128,32,128]{4,2,3,1,0:T(8,128)(2,1)}) fusion(bf16[8,4,128,32,128]{4,2,3,1,0:T(8,128)(2,1)} %all-to-all-done), kind=kLoop, calls=%fused_computation.153 | loop fusion | bytes 67108864 | tf_op jit(solution)/shard_map/slice | solution.py:79
  829.1 13.0 gather_fusion.1
  842.1 8.5 broadcast_select_fusion.1
  850.7 14.9 copy_select_fusion.2
  865.6 13.2 gather_fusion.2
  878.8 8.5 broadcast_select_fusion
  887.4 14.9 copy_select_fusion.1
  902.3 28.2 %pad_maximum_fusion = bf16[2,4,4,128,4,8,128]{6,2,1,5,3,0,4:T(4,128)(2,1)} fusion(bf16[1,4,4,128,4,8,128]{6,2,1,5,3,0,4:T(4,128)(2,1)} %copy_select_fusion.1, bf16[1,4,4,128,4,8,128]{6,2,1,5,3,0,4:T(4,128)(2,1)} %copy_select_fusion.2), kind=kLoop, calls=%fused_computation.16 | loop fusion | flops 16777216 | bytes 67108864 | tf_op jit(solution)/shard_map/stack | solution.py:83
  930.5 9.7 all-to-all-start.1
  940.2 0.2 all-reduce.4.cloned.1.call-start
  940.6 5.8 while.7
  940.6 0.7 constant_dynamic-slice_fusion.9
  941.2 0.8 dynamic-slice_bitcast_fusion.5
  942.0 0.7 constant_dynamic-slice_fusion.9
  942.7 0.8 dynamic-slice_bitcast_fusion.5
  943.5 0.7 constant_dynamic-slice_fusion.9
  944.2 0.8 dynamic-slice_bitcast_fusion.5
  945.0 0.7 constant_dynamic-slice_fusion.9
  945.6 0.8 dynamic-slice_bitcast_fusion.5
  946.4 5.3 while.6
  946.4 0.6 constant_dynamic-slice_fusion.8
  947.0 0.7 dynamic-slice_bitcast_fusion.4
  947.8 0.6 constant_dynamic-slice_fusion.8
  948.4 0.7 dynamic-slice_bitcast_fusion.4
  949.1 0.6 constant_dynamic-slice_fusion.8
  949.7 0.7 dynamic-slice_bitcast_fusion.4
  950.4 0.6 constant_dynamic-slice_fusion.8
  951.0 0.7 dynamic-slice_bitcast_fusion.4
  951.8 0.5 convert_reduce_fusion
  952.3 0.4 and_reduce_fusion.1
  952.6 0.4 fusion.12
  953.0 0.3 fusion.22
  953.3 0.4 and_reduce_fusion.3
  953.6 0.4 fusion.10
  954.0 0.3 fusion.24
  954.3 0.4 and_reduce_fusion
  954.6 0.4 fusion.13
  955.1 0.4 and_reduce_fusion.2
  955.5 0.4 fusion.11
  955.9 0.6 add_compare_fusion.1
  956.5 346.6 %all-to-all-done.1 = bf16[2,4,4,128,4,8,128]{6,2,1,5,3,0,4:T(4,128)(2,1)} async-done(((bf16[2,4,4,128,4,8,128]{6,2,1,5,3,0,4:T(4,128)(2,1)}), bf16[2,4,4,128,4,8,128]{6,2,1,5,3,0,4:T(4,128)(2,1)}, u32[]{:S(2)}, u32[]{:S(2)}) %all-to-all-start.1) | async-done | bytes 33554464 | tf_op jit(solution)/shard_map/all_to_all | solution.py:83
  1303.1 28.3 %fusion.45 = (bf16[1,4,4,128,4,8,128]{6,2,1,5,3,0,4:T(4,128)(2,1)}, bf16[1,4,4,128,4,8,128]{6,2,1,5,3,0,4:T(4,128)(2,1)}) fusion(bf16[2,4,4,128,4,8,128]{6,2,1,5,3,0,4:T(4,128)(2,1)} %all-to-all-done.1), kind=kLoop, calls=%fused_computation.152 | loop fusion | bytes 67108864 | tf_op jit(solution)/shard_map/slice | solution.py:105
  1331.3 21.2 %bitcast_convert_fusion = bf16[24,128,4,8,128]{4,0,3,2,1:T(8,128)(2,1)} fusion(bf16[1,4,4,128,4,8,128]{6,2,1,5,3,0,4:T(4,128)(2,1)} %get-tuple-element.95, s32[4,4]{1,0:T(4,128)S(1)} %fusion.22), kind=kOutput, calls=%fused_computation.12 | convolution fusion | flops 415236480 | bytes 41943104 | tf_op jit(solution)/shard_map/hsI,hsiatj->Iiatj/dot_general | solution.py:102
  1352.5 21.3 %bitcast_convert_fusion.1 = bf16[24,128,4,8,128]{4,0,3,2,1:T(8,128)(2,1)} fusion(bf16[1,4,4,128,4,8,128]{6,2,1,5,3,0,4:T(4,128)(2,1)} %get-tuple-element.96, s32[4,4]{1,0:T(4,128)S(1)} %fusion.24), kind=kOutput, calls=%fused_computation.13 | convolution fusion | flops 415236480 | bytes 41943104 | tf_op jit(solution)/shard_map/hsI,hsiatj->Iiatj/dot_general | solution.py:102
  1373.9 34.1 %fusion.5 = f32[24,128,128,48,1]{2,3,4,1,0:T(8,128)} fusion(bf16[24,128,4,8,128]{4,0,3,2,1:T(8,128)(2,1)} %bitcast_convert_fusion.1, s32[4,8]{1,0:T(4,128)S(1)} %bitcast.142), kind=kOutput, calls=%fused_computation.20 | convolution fusion | flops 1207961088 | bytes 100663424 | tf_op jit(solution)/shard_map/atJ,Iiatj->IiJj/dot_general | solution.py:108
  1408.0 45.4 %fusion.2 = bf16[24,128,128,48]{2,3,1,0:T(8,128)(2,1)} fusion(f32[24,128,128,48,1]{2,3,4,1,0:T(8,128)} %fusion.5, bf16[24,128,4,8,128]{4,0,3,2,1:T(8,128)(2,1)} %bitcast_convert_fusion, s32[4,8]{1,0:T(4,128)S(1)} %bitcast.141), kind=kOutput, calls=%fused_computation.11 | convolution fusion | flops 1245709824 | bytes 138412160 | tf_op jit(solution)/shard_map/atJ,Iiatj->IiJj/dot_general | solution.py:108
  1453.4 26.1 %copy.72 = bf16[384,8,48,128]{3,1,2,0:T(8,128)(2,1)} copy(bf16[384,8,48,128]{3,2,1,0:T(8,128)(2,1)} %bitcast.130) | data formatting | bytes 75497472
  1479.5 7.6 broadcast_select_fusion.2
  1487.2 8.0 slice_select_fusion
  1495.2 11.2 copy.73
  1506.5 0.8 dynamic-slice_convert_fusion
  1507.3 73.1 %all-reduce.4.cloned.1.call-done = bf16[3072,768]{1,0:T(8,128)(2,1)} async-done(((bf16[3072,768]{1,0:T(8,128)(2,1)}), bf16[3072,768]{1,0:T(8,128)(2,1)}) %all-reduce.4.cloned.1.call-update) | async-done | bytes 4718608 | tf_op jit(solution)/shard_map/psum | solution.py:13
  1580.4 299.9 %all-reduce.6.cloned.1.call-done = bf16[768,6144]{1,0:T(8,128)(2,1)} async-done(((bf16[768,6144]{1,0:T(8,128)(2,1)}), bf16[768,6144]{1,0:T(8,128)(2,1)}) %all-reduce.6.cloned.1.call-update) | async-done | bytes 9437200 | tf_op jit(solution)/shard_map/psum | solution.py:13
  1880.3 24.2 %mul.58 = f32[24,128,48,128]{3,2,1,0:T(8,128)} broadcast(f32[24,48]{1,0:T(8,128)S(1)} %dynamic-slice_convert_fusion), dimensions={0,2} | broadcast | bytes 75502080 | tf_op jit(solution)/shard_map/mul | solution.py:122
  1904.5 79.2 %select_select_fusion = bf16[3072,6144]{1,0:T(8,128)(2,1)} fusion(bf16[3072,768]{1,0:T(8,128)(2,1)} %all-reduce.4.cloned.1.call-done, pred[3072]{0:T(1024)(128)(4,1)S(1)} %copy-done.1, pred[6144]{0:T(1024)(128)(4,1)S(1)} %add_compare_fusion, f32[384,8,48,128]{3,2,1,0:T(8,128)} %bitcast.64, bf16[768,6144]{1,0:T(8,128)(2,1)} %all-reduce.6.cloned.1.call-done, ...), kind=kOutput, calls=%fused_computation.15 | convolution fusion | flops 29104275456 | bytes 165159936 | tf_op jit(solution)/shard_map/dot_general | solution.py:121
  (65 shorter events, 2.3 us)
Async XLA Ops:
  6.5 1472.9 %copy-start = (bf16[768,768]{1,0:T(8,128)(2,1)S(1)}, bf16[768,768]{1,0:T(8,128)(2,1)}, u32[]{:S(2)}) copy-start(bf16[768,768]{1,0:T(8,128)(2,1)} %param.9) | copy-start | bytes 3538948
  77.0 7.2 copy-start.2
  77.0 728.6 %all-to-all-start = ((bf16[8,4,128,32,128]{4,2,3,1,0:T(8,128)(2,1)}), bf16[8,4,128,32,128]{4,2,3,1,0:T(8,128)(2,1)}, u32[]{:S(2)}, u32[]{:S(2)}) async-start(bf16[8,4,128,32,128]{4,2,3,1,0:T(8,128)(2,1)} %fusion.3), calls=%async_computation | async-start | bytes 67108864 | tf_op jit(solution)/shard_map/all_to_all | solution.py:74
  930.5 372.6 %all-to-all-start.1 = ((bf16[2,4,4,128,4,8,128]{6,2,1,5,3,0,4:T(4,128)(2,1)}), bf16[2,4,4,128,4,8,128]{6,2,1,5,3,0,4:T(4,128)(2,1)}, u32[]{:S(2)}, u32[]{:S(2)}) async-start(bf16[2,4,4,128,4,8,128]{6,2,1,5,3,0,4:T(4,128)(2,1)} %pad_maximum_fusion), calls=%async_computation.1 | async-start | bytes 67108864 | tf_op jit(solution)/shard_map/all_to_all | solution.py:83
  940.2 640.1 %all-reduce.4.cloned.1.call-start = ((), (), s32[]{:S(2)}) async-start(), calls=%async_computation.2 | async-start | bytes 9437184 | tf_op jit(solution)/shard_map/psum | solution.py:13
  1453.4 26.1 %copy-start.1 = (pred[3072]{0:T(1024)(128)(4,1)S(1)}, pred[3072]{0:T(1024)(128)(4,1)}, u32[]{:S(2)}) copy-start(pred[3072]{0:T(1024)(128)(4,1)} %add_compare_fusion.1) | copy-start | bytes 9220
  1487.1 393.2 %all-reduce.6.cloned.1.call-start = ((), (), s32[]{:S(2)}) async-start(), calls=%async_computation.3 | async-start | bytes 18874368 | tf_op jit(solution)/shard_map/psum | solution.py:13
Sparse Core Ops, SparseCore 0:
  1487.2 93.0 all-reduce.3
  1584.2 296.0 all-reduce.5
where the time goes:
time: 2000 us; the launch traced here: 1990 us
  waiting for transfers between devices  1440 us (72%)
  matrix products  209 us (10%)
  local copies, waits for them, and re-layouts  197 us (10%)
  other arithmetic  114 us (6%)
    all_to_all x1, waiting for transfers between devices, body(): lax.all_to_all(by_rows, 'row', split_axis=0, concat_axis=0, tiled=True)  720 us
    psum x2, waiting for transfers between devices, broadcast(): return lax.psum(jnp.where(mine, x, jnp.zeros_like(x)), axis)  373 us
    all_to_all x1, waiting for transfers between devices, body(): lax.all_to_all(jnp.stack(stacked), 'col', split_axis=4, concat_axis=4, ti...  347 us
    dot_general x2, matrix products, body(): jnp.einsum('atJ,Iiatj->IiJj', col_pick, placed, preferred_element_type=jn...  79.5 us
    dot_general x1, matrix products, body(): update = jnp.dot(lower, upper, preferred_element_type=jnp.float32)  79.2 us
    unnamed x11, local copies, waits for them, and re-layouts  60.4 us
    dot_general x2, matrix products, body(): jnp.einsum('hsI,' + layout + '->Iiatj', row_pick, arrived[child_id], pref...  42.6 us
  transfers between devices with their start and end apart: 4, of which 4 were waited for; matrix products, arithmetic and copies ran while one was open for 2% of the time, Pallas kernels for 0%

commit v1 on v0

v1 whole, which is shorter than its diff:
```python
import functools

import jax
import jax.numpy as jnp
from jax import lax
from jax.experimental import pallas as pl
from jax.experimental.pallas import tpu as pltpu
from jax.sharding import PartitionSpec as P

CB = 128
MESH = pl.DeviceIdType.MESH
VMEM_LIMIT = 56 * 1024 * 1024


def ranks(child_map, run, owned):
    count = child_map.shape[1]
    target = child_map // owned
    places = jnp.arange(count, dtype=jnp.int32)
    same = (target[:, :, None] == target[:, None, :]) & (
        (places[:, None] // run == places[None, :] // run) & (places[None, :] < places[:, None])
    )[None]
    return jnp.sum(same.astype(jnp.int32), axis=2)


def send_table(child_map, rank, child, start, run, owned, dests, cap):
    parents = lax.dynamic_slice(child_map, (child, start), (1, run))[0]
    rank = lax.dynamic_slice(rank, (child, start), (1, run))[0]
    slot = (parents // owned) * cap + rank
    hits = slot[None, :] == jnp.arange(dests * cap, dtype=jnp.int32)[:, None]
    return jnp.sum(jnp.where(hits, jnp.arange(run, dtype=jnp.int32)[None, :], 0), axis=1)


def receive_table(child_map, rank, mine, run, owned):
    count = child_map.shape[1]
    wanted = mine * owned + jnp.arange(owned, dtype=jnp.int32)
    hits = child_map[:, None, :] == wanted[None, :, None]
    shard = jnp.arange(count, dtype=jnp.int32) // run
    shard = jnp.sum(jnp.where(hits, shard[None, None, :], 0), axis=2)
    slot = jnp.sum(jnp.where(hits, rank[:, None, :], 0), axis=2)
    return shard, slot, jnp.any(hits, axis=2).astype(jnp.int32)


def pack_kernel(dests, slots, row_src, col_src, x_ref, o_ref):
    for c in range(dests):
        for t in range(slots):
            at = pl.multiple_of(col_src[c * slots + t] * CB, CB)
            o_ref[0, c, 0, :, t * CB : (t + 1) * CB] = x_ref[:, pl.ds(at, CB)]


def front_tile(tiles, flags, col_tab, own_cols, col):
    total = None
    for k in range(2):
        a = col_tab[(0 + k) * own_cols + col]
        t = pl.multiple_of(col_tab[(2 + k) * own_cols + col] * CB, CB)
        there = (flags[k] * col_tab[(4 + k) * own_cols + col]).astype(jnp.float32)
        part = tiles[k][0, a, 0, :, pl.ds(t, CB)].astype(jnp.float32) * there
        total = part if total is None else total + part
    return total.astype(jnp.bfloat16)


def row_flags(row_tab, own_rows, row):
    return [row_tab[(4 + k) * own_rows + row] for k in range(2)]


def upper_kernel(own_rows, own_cols, row_tab, col_tab, t0, t1, o_ref):
    flags = row_flags(row_tab, own_rows, pl.program_id(0))
    for j in range(own_cols):
        o_ref[:, j * CB : (j + 1) * CB] = front_tile((t0, t1), flags, col_tab, own_cols, j)


def lower_kernel(own_rows, own_cols, group, panel, row_tab, col_tab, place, *refs):
    tiles, (inv_ref, o_ref, held) = refs[: 2 * group], refs[2 * group :]
    for r in range(group):
        row = pl.program_id(0) * group + r
        flags = row_flags(row_tab, own_rows, row)
        for j in range(panel):
            held[r * CB : (r + 1) * CB, j * CB : (j + 1) * CB] = front_tile(
                tiles[2 * r : 2 * r + 2], flags, col_tab, own_cols, j
            )
    lower = jnp.dot(held[...], inv_ref[...], preferred_element_type=jnp.float32)
    for r in range(group):
        row = place[0] * own_rows + pl.program_id(0) * group + r
        below = (row >= panel).astype(jnp.float32)
        o_ref[r * CB : (r + 1) * CB, :] = (lower[r * CB : (r + 1) * CB] * below).astype(jnp.bfloat16)


def final_kernel(own_rows, own_cols, group, panel, wide, row_tab, col_tab, place, keep, *refs):
    tiles, (lower_ref, upper_ref, o_ref) = refs[: 2 * group], refs[2 * group :]
    rows = [pl.program_id(0) * group + r for r in range(group)]
    flags = [row_flags(row_tab, own_rows, row) for row in rows]

    def step(n, carry):
        at = pl.multiple_of(n * (wide * CB), wide * CB)
        update = jnp.dot(
            lower_ref[...], upper_ref[:, pl.ds(at, wide * CB)], preferred_element_type=jnp.float32
        )
        for q in range(wide):
            col = n * wide + q
            for r in range(group):
                front = front_tile(tiles[2 * r : 2 * r + 2], flags[r], col_tab, own_cols, col)
                mask = keep[rows[r] * own_cols + col].astype(jnp.float32)
                part = update[r * CB : (r + 1) * CB, q * CB : (q + 1) * CB] * mask
                o_ref[r * CB : (r + 1) * CB, pl.ds(pl.multiple_of(at + q * CB, CB), CB)] = (
                    front.astype(jnp.float32) - part
                ).astype(jnp.bfloat16)
        return carry

    lax.fori_loop(0, own_cols // wide, step, 0)
    for r in range(group):

        @pl.when((place[1] == 0) & (place[0] * own_rows + rows[r] >= panel))
        def _():
            o_ref[r * CB : (r + 1) * CB, : panel * CB] = lower_ref[r * CB : (r + 1) * CB, :]


def spread_kernel(n, m, chunks, u_in, l_in, upper, lower, down, across, first, line, other, l_send, l_recv):
    row, col = lax.axis_index("row"), lax.axis_index("col")
    high, low = row // 2, row % 2
    barrier = pltpu.get_barrier_semaphore()
    for off in range(1, n):
        pl.semaphore_signal(barrier, inc=1, device_id=(lax.rem(row + off, n), col), device_id_type=MESH)
    for off in range(1, m):
        pl.semaphore_signal(barrier, inc=1, device_id=(row, lax.rem(col + off, m)), device_id_type=MESH)
    pl.semaphore_wait(barrier, n + m - 2)

    depth = upper.shape[0] // (2 * chunks)
    root = row == 0
    partner = high * 2 + (1 - low)
    goes_down = row + 2 < n
    goes_across = row != 1

    def move(half, c, send, recv, to):
        at = pl.multiple_of((half * chunks + c) * depth, depth)
        part = upper.at[pl.ds(at, depth), :]
        return pltpu.make_async_remote_copy(
            src_ref=part, dst_ref=part, send_sem=send.at[c], recv_sem=recv.at[c],
            device_id=(to, col), device_id_type=MESH,
        )

    def move_lower(p):
        return pltpu.make_async_remote_copy(
            src_ref=lower, dst_ref=lower, send_sem=l_send.at[p - 1], recv_sem=l_recv,
            device_id=(row, p), device_id_type=MESH,
        )

    for p in range(m - 1, 0, -1):

        @pl.when(col == 0)
        def _():
            move_lower(p).start()

    def send(c, carry):
        @pl.when(row != 0)
        def _():
            move(low, c, down, line, partner).wait_recv()

        @pl.when(goes_down)
        def _():
            move(low, c, down, line, row + 2).start()

        @pl.when(root)
        def _():
            move(1, c, first, line, 1).start()

        @pl.when(goes_across)
        def _():
            move(low, c, across, other, partner).start()

        return carry

    lax.fori_loop(0, chunks, send, 0)

    def finish(c, carry):
        @pl.when(row != 0)
        def _():
            move(1 - low, c, across, other, partner).wait_recv()

        @pl.when(goes_down)
        def _():
            move(low, c, down, line, row + 2).wait_send()

        @pl.when(root)
        def _():
            move(1, c, first, line, 1).wait_send()

        @pl.when(goes_across)
        def _():
            move(low, c, across, other, partner).wait_send()

        return carry

    lax.fori_loop(0, chunks, finish, 0)

    @pl.when(col != 0)
    def _():
        move_lower(1).wait_recv()

    for p in range(1, m):

        @pl.when(col == 0)
        def _():
            move_lower(p).wait_send()


def spread(upper, lower, n, m):
    chunks = 12
    dma = pltpu.SemaphoreType.DMA
    anywhere = pl.BlockSpec(memory_space=pl.ANY)
    return pl.pallas_call(
        functools.partial(spread_kernel, n, m, chunks),
        out_shape=(
            jax.ShapeDtypeStruct(upper.shape, upper.dtype),
            jax.ShapeDtypeStruct(lower.shape, lower.dtype),
        ),
        in_specs=[anywhere] * 2,
        out_specs=(anywhere, anywhere),
        scratch_shapes=[dma((chunks,))] * 5 + [dma((m - 1,)), dma],
        input_output_aliases={0: 0, 1: 1},
        compiler_params=pltpu.CompilerParams(collective_id=0, has_side_effects=True),
    )(upper, lower)


def body(child_update, child_map, tile_mask, diag_inverse):
    n, m = lax.axis_size("row"), lax.axis_size("col")
    row_index, col_index = lax.axis_index("row"), lax.axis_index("col")
    per_child = n // 2
    blocks = child_map.shape[1]
    row_blocks, col_blocks = child_update.shape[0] // CB, child_update.shape[1] // CB
    own_rows, own_cols = tile_mask.shape[0] // n, tile_mask.shape[1] // m
    width = diag_inverse.shape[0]
    panel = width // CB
    cap_rows = 2 * (16 // n) * max(1, 8 // n)
    cap_cols = blocks // (m * m)
    child, within = row_index // per_child, row_index % per_child

    row_rank = ranks(child_map, row_blocks, own_rows)
    col_rank = ranks(child_map, col_blocks, own_cols)
    row_src = send_table(child_map, row_rank, child, within * row_blocks, row_blocks, own_rows, n, cap_rows)
    col_src = send_table(child_map, col_rank, child, col_index * col_blocks, col_blocks, own_cols, m, cap_cols)
    shard, slot, there = receive_table(child_map, row_rank, row_index, row_blocks, own_rows)
    shard = shard + per_child * jnp.arange(2, dtype=jnp.int32)[:, None]
    row_tab = jnp.concatenate([shard, slot, there]).reshape(-1)
    col_tab = jnp.concatenate(receive_table(child_map, col_rank, col_index, col_blocks, own_cols)).reshape(-1)
    place = jnp.stack([row_index, col_index]).astype(jnp.int32)
    keep = lax.dynamic_slice(
        tile_mask, (row_index * own_rows, col_index * own_cols), (own_rows, own_cols)
    ).reshape(-1)

    params = pltpu.CompilerParams(vmem_limit_bytes=VMEM_LIMIT)
    tile_block = (1, m, 1, CB, cap_cols * CB)
    packed = pl.pallas_call(
        functools.partial(pack_kernel, m, cap_cols),
        grid_spec=pltpu.PrefetchScalarGridSpec(
            num_scalar_prefetch=2,
            grid=(n * cap_rows,),
            in_specs=[pl.BlockSpec((CB, col_blocks * CB), lambda g, rs, cs: (rs[g], 0))],
            out_specs=pl.BlockSpec(tile_block, lambda g, rs, cs: (g // cap_rows, 0, g % cap_rows, 0, 0)),
        ),
        out_shape=jax.ShapeDtypeStruct((n, m, cap_rows, CB, cap_cols * CB), jnp.bfloat16),
        compiler_params=params,
    )(row_src, col_src, child_update)
    arrived = lax.all_to_all(
        packed.reshape(n * m, cap_rows, CB, cap_cols * CB), ("row", "col"), split_axis=0, concat_axis=0, tiled=True
    ).reshape(packed.shape)

    def tile_specs(group):
        def spec(r, k):
            def where(g, row_tab, *_):
                row = g * group + r
                return (row_tab[k * own_rows + row], 0, row_tab[(2 + k) * own_rows + row], 0, 0)

            return pl.BlockSpec(tile_block, where)

        return [spec(r, k) for r in range(group) for k in range(2)]

    upper = pl.pallas_call(
        functools.partial(upper_kernel, own_rows, own_cols),
        grid_spec=pltpu.PrefetchScalarGridSpec(
            num_scalar_prefetch=2,
            grid=(panel,),
            in_specs=tile_specs(1),
            out_specs=pl.BlockSpec((CB, own_cols * CB), lambda g, *_: (g, 0)),
        ),
        out_shape=jax.ShapeDtypeStruct((width, own_cols * CB), jnp.bfloat16),
        compiler_params=params,
    )(row_tab, col_tab, arrived, arrived)

    group = 2
    lower = pl.pallas_call(
        functools.partial(lower_kernel, own_rows, own_cols, group, panel),
        grid_spec=pltpu.PrefetchScalarGridSpec(
            num_scalar_prefetch=3,
            grid=(own_rows // group,),
            in_specs=tile_specs(group) + [pl.BlockSpec((width, width), lambda g, *_: (0, 0))],
            out_specs=pl.BlockSpec((group * CB, width), lambda g, *_: (g, 0)),
            scratch_shapes=[pltpu.VMEM((group * CB, width), jnp.bfloat16)],
        ),
        out_shape=jax.ShapeDtypeStruct((own_rows * CB, width), jnp.bfloat16),
        compiler_params=params,
    )(row_tab, col_tab, place, *([arrived] * (2 * group)), diag_inverse)

    upper, lower = spread(upper, lower, n, m)

    return pl.pallas_call(
        functools.partial(final_kernel, own_rows, own_cols, group, panel, 4),
        grid_spec=pltpu.PrefetchScalarGridSpec(
            num_scalar_prefetch=4,
            grid=(own_rows // group,),
            in_specs=tile_specs(group)
            + [
                pl.BlockSpec((group * CB, width), lambda g, *_: (g, 0)),
                pl.BlockSpec((width, own_cols * CB), lambda g, *_: (0, 0)),
            ],
            out_specs=pl.BlockSpec((group * CB, own_cols * CB), lambda g, *_: (g, 0)),
        ),
        out_shape=jax.ShapeDtypeStruct((own_rows * CB, own_cols * CB), jnp.bfloat16),
        compiler_params=params,
    )(row_tab, col_tab, place, keep, *([arrived] * (2 * group)), lower, upper)


def solution(mesh):
    placed = (P("row", "col"), P(), P(), P())
    return jax.shard_map(
        body, mesh=mesh, in_specs=placed, out_specs=P("row", "col"), check_vma=False
    )
```

time: 2000 us -> 1140 us (0.57)
  waiting for transfers between devices: 1440 us -> 719 us
  Pallas kernels: 0 us -> 406 us
  matrix products: 209 us -> 0 us
  local copies, waits for them, and re-layouts: 197 us -> 2.83 us
  other arithmetic: 114 us -> 4.06 us
    pallas_call x0 -> x5, Pallas kernels: none -> 406 us  [the longest x1 259 us: spread(): pl.pallas_call(functools.partial(spread_kernel, n, m, chunks), out_shape=...]
    psum x2 -> x0, waiting for transfers between devices: 373 us -> none  [broadcast(): return lax.psum(jnp.where(mine, x, jnp.zeros_like(x)), axis)]
    all_to_all x2 -> x1, waiting for transfers between devices: 1070 us -> 719 us  [body(): lax.all_to_all(packed.reshape(n * m, cap_rows, CB, cap_cols * CB), ('row'...]
    dot_general x6 -> x0, matrix products: 209 us -> none  [the longest x2 79.5 us: body(): jnp.einsum('atJ,Iiatj->IiJj', col_pick, placed, preferred_element_type=jn...]
    select_n x13 -> x2, other arithmetic: 78.7 us -> 0.69 us  [the longest x1 0.69 us: ranks(): target = child_map // owned]
    unnamed x11 -> x2, local copies, waits for them, and re-layouts: 60.4 us -> 0.01 us
    gather x27 -> x0, local copies, waits for them, and re-layouts: 60.2 us -> none  [the longest x2 26.3 us: body(): jnp.take(arrived_rows[child_id], col_source.reshape(-1), axis=3)]
    slice x2 -> x0, local copies, waits for them, and re-layouts: 51.8 us -> none  [the longest x1 28.3 us: body(): arrived[child_id]]
  transfers between devices with their start and end apart: 4 -> 1, of which waited for: 4 -> 1; matrix products, arithmetic and copies ran while one was open for 2% -> 0% of each run, Pallas kernels for 0% -> 0%
where the time goes in v1:
time: 1140 us
  waiting for transfers between devices  719 us (63%)
  Pallas kernels  406 us (36%)
    all_to_all x1, waiting for transfers between devices, body(): lax.all_to_all(packed.reshape(n * m, cap_rows, CB, cap_cols * CB), ('row'...  719 us
    pallas_call x1, Pallas kernels, spread(): pl.pallas_call(functools.partial(spread_kernel, n, m, chunks), out_shape=...  259 us
    pallas_call x1, Pallas kernels, body(): pl.pallas_call(functools.partial(final_kernel, own_rows, own_cols, group,...  75.1 us
    pallas_call x1, Pallas kernels, body(): pl.pallas_call(functools.partial(pack_kernel, m, cap_cols), grid_spec=plt...  38 us
  transfers between devices with their start and end apart: 1, of which 1 were waited for; matrix products, arithmetic and copies ran while one was open for 0% of the time, Pallas kernels for 0%

profile of v1, /device:TPU:24, one launch (start us, length us, event | category | flops | bytes accessed | tf_op | source)
XLA Modules:
  0.0 1138.2 jit_solution(9813726232359031075)
XLA Ops:
  0.0 0.7 and_select_fusion.3
  0.7 0.1 fusion
  0.8 0.2 convert_reduce_fusion
  1.0 0.8 add_bitcast_fusion
  1.9 0.7 select_reduce_fusion
  2.6 38.0 %shard_map.46 = bf16[8,4,4,128,1024]{4,3,2,1,0:T(8,128)(2,1)} custom-call(s32[32]{0:T(128)} %get-tuple-element.20.row_src, s32[32]{0:T(128)} %get-tuple-element.19.col_src, bf16[4096,4096]{1,0:T(8,128)(2,1)} %x_ref.1), custom_call_target="tpu_custom_call" | custom-call | tf_op jit(solution)/shard_map/pallas_call | solution.py:251
  40.6 0.0 copy-start
  40.6 5.9 all-to-all-start
  46.5 0.0 copy-done
  46.5 0.2 compare_reduce_fusion
  46.8 0.2 compare_reduce_fusion.1
  46.9 0.8 dynamic_slice.15
  47.8 0.7 reshape.164.keep
  48.4 0.2 fusion.1
  48.7 0.7 reshape.163.col_tab
  49.3 0.2 fusion.3
  49.5 0.1 broadcast_add_fusion
  49.6 0.7 reshape.162.row_tab
  50.3 0.6 pad_add_fusion.2.place
  50.9 718.9 %all-to-all-done = bf16[32,4,128,1024]{3,2,1,0:T(8,128)(2,1)} async-done(((bf16[32,4,128,1024]{3,2,1,0:T(8,128)(2,1)}), bf16[32,4,128,1024]{3,2,1,0:T(8,128)(2,1)}, u32[]{:S(2)}, u32[]{:S(2)}) %all-to-all-start) | async-done | bytes 33554464 | tf_op jit(solution)/shard_map/all_to_all | solution.py:262
  769.8 12.2 %shard_map.47.u_in = bf16[768,6144]{1,0:T(8,128)(2,1)} custom-call(s32[144]{0:T(256)} %reshape.162.row_tab, s32[288]{0:T(512)} %reshape.163.col_tab, bf16[8,4,4,128,1024]{4,3,2,1,0:T(8,128)(2,1)} %bitcast.5.t0.t1.refs_0_.refs_1_.refs_2_.refs_3_, bf16[8,4,4,128,1024]{4,3,2,1,0:T(8,128)(2,1)} %bitcast.5.t0.t1.refs_0_.refs_1_.refs_2_.refs_3_), custom_call_target="tpu_custom_call" | custom-call | tf_op jit(solution)/shard_map/pallas_call | solution.py:276
  782.0 22.0 %shard_map.48.l_in = bf16[3072,768]{1,0:T(8,128)(2,1)} custom-call(s32[144]{0:T(256)} %reshape.162.row_tab, s32[288]{0:T(512)} %reshape.163.col_tab, s32[2]{0:T(128)} %pad_add_fusion.2.place, bf16[8,4,4,128,1024]{4,3,2,1,0:T(8,128)(2,1)} %bitcast.5.t0.t1.refs_0_.refs_1_.refs_2_.refs_3_, ...), custom_call_target="tpu_custom_call" | custom-call | tf_op jit(solution)/shard_map/pallas_call | solution.py:289
  803.9 259.1 %shard_map.49 = (bf16[768,6144]{1,0:T(8,128)(2,1)}, bf16[3072,768]{1,0:T(8,128)(2,1)}) custom-call(bf16[768,6144]{1,0:T(8,128)(2,1)} %shard_map.47.u_in, bf16[3072,768]{1,0:T(8,128)(2,1)} %shard_map.48.l_in), custom_call_target="tpu_custom_call", output_to_operand_aliasing={{0}: (0, {}), {1}: (1, {})} | custom-call | tf_op jit(solution)/shard_map/pallas_call | solution.py:209
  1063.1 75.1 %shard_map.50 = bf16[3072,6144]{1,0:T(8,128)(2,1)} custom-call(s32[144]{0:T(256)} %reshape.162.row_tab, s32[288]{0:T(512)} %reshape.163.col_tab, s32[2]{0:T(128)} %pad_add_fusion.2.place, s32[1152]{0:T(1024)} %reshape.164.keep, bf16[8,4,4,128,1024]{4,3,2,1,0:T(8,128)(2,1)} %bitcast.5.t0.t1.refs_0_.refs_1_.refs_2_.refs_3_, ...), custom_call_target="tpu_custom_call" | custom-call | tf_op jit(solution)/shard_map/pallas_call | solution.py:304
  (8 shorter events, 0.1 us)
Async XLA Ops:
  40.6 5.9 copy-start
  40.6 729.2 %all-to-all-start = ((bf16[32,4,128,1024]{3,2,1,0:T(8,128)(2,1)}), bf16[32,4,128,1024]{3,2,1,0:T(8,128)(2,1)}, u32[]{:S(2)}, u32[]{:S(2)}) async-start(bf16[32,4,128,1024]{3,2,1,0:T(8,128)(2,1)} %bitcast.8), calls=%async_computation | async-start | bytes 67108864 | tf_op jit(solution)/shard_map/all_to_all | solution.py:262

commit v2 on v1

--- a/solution.py
+++ b/solution.py
@@ -40,11 +40,12 @@
     return shard, slot, jnp.any(hits, axis=2).astype(jnp.int32)
 
 
-def pack_kernel(dests, slots, row_src, col_src, x_ref, o_ref):
+def pack_kernel(dests, slots, row_src, col_src, x0_ref, x1_ref, o_ref):
     for c in range(dests):
         for t in range(slots):
             at = pl.multiple_of(col_src[c * slots + t] * CB, CB)
-            o_ref[0, c, 0, :, t * CB : (t + 1) * CB] = x_ref[:, pl.ds(at, CB)]
+            for i, x_ref in enumerate((x0_ref, x1_ref)):
+                o_ref[0, c, i, :, t * CB : (t + 1) * CB] = x_ref[:, pl.ds(at, CB)]
 
 
 def front_tile(tiles, flags, col_tab, own_cols, col):
@@ -53,9 +54,10 @@
         a = col_tab[(0 + k) * own_cols + col]
         t = pl.multiple_of(col_tab[(2 + k) * own_cols + col] * CB, CB)
         there = (flags[k] * col_tab[(4 + k) * own_cols + col]).astype(jnp.float32)
-        part = tiles[k][0, a, 0, :, pl.ds(t, CB)].astype(jnp.float32) * there
+        there = jnp.full((CB, CB), there, jnp.float32).astype(jnp.bfloat16)
+        part = tiles[k][0, a, 0, :, pl.ds(t, CB)] * there
         total = part if total is None else total + part
-    return total.astype(jnp.bfloat16)
+    return total
 
 
 def row_flags(row_tab, own_rows, row):
@@ -90,7 +92,7 @@
     flags = [row_flags(row_tab, own_rows, row) for row in rows]
 
     def step(n, carry):
-        at = pl.multiple_of(n * (wide * CB), wide * CB)
+        at = n * (wide * CB)
         update = jnp.dot(
             lower_ref[...], upper_ref[:, pl.ds(at, wide * CB)], preferred_element_type=jnp.float32
         )
@@ -100,12 +102,13 @@
                 front = front_tile(tiles[2 * r : 2 * r + 2], flags[r], col_tab, own_cols, col)
                 mask = keep[rows[r] * own_cols + col].astype(jnp.float32)
                 part = update[r * CB : (r + 1) * CB, q * CB : (q + 1) * CB] * mask
-                o_ref[r * CB : (r + 1) * CB, pl.ds(pl.multiple_of(at + q * CB, CB), CB)] = (
+                o_ref[r * CB : (r + 1) * CB, pl.ds(at + q * CB, CB)] = (
                     front.astype(jnp.float32) - part
                 ).astype(jnp.bfloat16)
         return carry
 
-    lax.fori_loop(0, own_cols // wide, step, 0)
+    for n in range(own_cols // wide):
+        step(n, 0)
     for r in range(group):
 
         @pl.when((place[1] == 0) & (place[0] * own_rows + rows[r] >= panel))
@@ -113,7 +116,7 @@
             o_ref[r * CB : (r + 1) * CB, : panel * CB] = lower_ref[r * CB : (r + 1) * CB, :]
 
 
-def spread_kernel(n, m, chunks, u_in, l_in, upper, lower, down, across, first, line, other, l_send, l_recv):
+def spread_kernel(n, m, chunks, u_in, l_in, upper, lower, down, across, first, line, other, up, l_send, l_recv):
     row, col = lax.axis_index("row"), lax.axis_index("col")
     high, low = row // 2, row % 2
     barrier = pltpu.get_barrier_semaphore()
@@ -127,7 +130,8 @@
     root = row == 0
     partner = high * 2 + (1 - low)
     goes_down = row + 2 < n
-    goes_across = row != 1
+    goes_across = (row != 1) & (row != 0)
+    goes_up = row == 3
 
     def move(half, c, send, recv, to):
         at = pl.multiple_of((half * chunks + c) * depth, depth)
@@ -149,6 +153,10 @@
         def _():
             move_lower(p).start()
 
+    def lift(c):
+        move(0, c, across, other, partner).wait_recv()
+        move(0, c, up, other, 1).start()
+
     def send(c, carry):
         @pl.when(row != 0)
         def _():
@@ -166,14 +174,26 @@
         def _():
             move(low, c, across, other, partner).start()
 
+        @pl.when(goes_up & (c > 0))
+        def _():
+            lift(c - 1)
+
         return carry
 
     lax.fori_loop(0, chunks, send, 0)
 
+    @pl.when(goes_up)
+    def _():
+        lift(chunks - 1)
+
     def finish(c, carry):
-        @pl.when(row != 0)
+        @pl.when((row != 0) & jnp.logical_not(goes_up))
         def _():
             move(1 - low, c, across, other, partner).wait_recv()
+
+        @pl.when(goes_up)
+        def _():
+            move(0, c, up, other, 1).wait_send()
 
         @pl.when(goes_down)
         def _():
@@ -203,7 +223,7 @@
 
 
 def spread(upper, lower, n, m):
-    chunks = 12
+    chunks = 24
     dma = pltpu.SemaphoreType.DMA
     anywhere = pl.BlockSpec(memory_space=pl.ANY)
     return pl.pallas_call(
@@ -214,7 +234,7 @@
         ),
         in_specs=[anywhere] * 2,
         out_specs=(anywhere, anywhere),
-        scratch_shapes=[dma((chunks,))] * 5 + [dma((m - 1,)), dma],
+        scratch_shapes=[dma((chunks,))] * 6 + [dma((m - 1,)), dma],
         input_output_aliases={0: 0, 1: 1},
         compiler_params=pltpu.CompilerParams(collective_id=0, has_side_effects=True),
     )(upper, lower)
@@ -252,13 +272,19 @@
         functools.partial(pack_kernel, m, cap_cols),
         grid_spec=pltpu.PrefetchScalarGridSpec(
             num_scalar_prefetch=2,
-            grid=(n * cap_rows,),
-            in_specs=[pl.BlockSpec((CB, col_blocks * CB), lambda g, rs, cs: (rs[g], 0))],
-            out_specs=pl.BlockSpec(tile_block, lambda g, rs, cs: (g // cap_rows, 0, g % cap_rows, 0, 0)),
+            grid=(n * cap_rows // 2,),
+            in_specs=[
+                pl.BlockSpec((CB, col_blocks * CB), lambda g, rs, cs: (rs[2 * g], 0)),
+                pl.BlockSpec((CB, col_blocks * CB), lambda g, rs, cs: (rs[2 * g + 1], 0)),
+            ],
+            out_specs=pl.BlockSpec(
+                (1, m, 2, CB, cap_cols * CB),
+                lambda g, rs, cs: (g // (cap_rows // 2), 0, g % (cap_rows // 2), 0, 0),
+            ),
         ),
         out_shape=jax.ShapeDtypeStruct((n, m, cap_rows, CB, cap_cols * CB), jnp.bfloat16),
         compiler_params=params,
-    )(row_src, col_src, child_update)
+    )(row_src, col_src, child_update, child_update)
     arrived = lax.all_to_all(
         packed.reshape(n * m, cap_rows, CB, cap_cols * CB), ("row", "col"), split_axis=0, concat_axis=0, tiled=True
     ).reshape(packed.shape)
@@ -285,7 +311,7 @@
         compiler_params=params,
     )(row_tab, col_tab, arrived, arrived)
 
-    group = 2
+    group = 4
     lower = pl.pallas_call(
         functools.partial(lower_kernel, own_rows, own_cols, group, panel),
         grid_spec=pltpu.PrefetchScalarGridSpec(

time: 1140 us -> 998 us (0.88)
  Pallas kernels: 406 us -> 266 us
    pallas_call x1, Pallas kernels: 259 us -> 151 us  [spread(): pl.pallas_call(functools.partial(spread_kernel, n, m, chunks), out_shape=...]
    pallas_call x1, Pallas kernels: 75.1 us -> 52.7 us  [body(): pl.pallas_call(functools.partial(final_kernel, own_rows, own_cols, group,...]
where the time goes in v2:
time: 998 us
  waiting for transfers between devices  719 us (72%)
  Pallas kernels  266 us (27%)
    all_to_all x1, waiting for transfers between devices, body(): lax.all_to_all(packed.reshape(n * m, cap_rows, CB, cap_cols * CB), ('row'...  719 us
    pallas_call x1, Pallas kernels, spread(): pl.pallas_call(functools.partial(spread_kernel, n, m, chunks), out_shape=...  151 us
    pallas_call x1, Pallas kernels, body(): pl.pallas_call(functools.partial(final_kernel, own_rows, own_cols, group,...  52.7 us
    pallas_call x1, Pallas kernels, body(): pl.pallas_call(functools.partial(pack_kernel, m, cap_cols), grid_spec=plt...  30.6 us
  transfers between devices with their start and end apart: 1, of which 1 were waited for; matrix products, arithmetic and copies ran while one was open for 0% of the time, Pallas kernels for 0%

profile of v2, /device:TPU:24, one launch (start us, length us, event | category | flops | bytes accessed | tf_op | source)
XLA Modules:
  0.0 997.6 jit_solution(796511523817163056)
XLA Ops:
  0.0 0.7 and_select_fusion.3
  0.7 0.1 fusion
  0.8 0.2 convert_reduce_fusion
  1.0 0.8 add_bitcast_fusion
  1.9 0.7 select_reduce_fusion
  2.6 30.6 %shard_map.46 = bf16[8,4,4,128,1024]{4,3,2,1,0:T(8,128)(2,1)} custom-call(s32[32]{0:T(128)} %get-tuple-element.20.row_src, s32[32]{0:T(128)} %get-tuple-element.19.col_src, bf16[4096,4096]{1,0:T(8,128)(2,1)} %x1_ref.1, bf16[4096,4096]{1,0:T(8,128)(2,1)} %x1_ref.1), custom_call_target="tpu_custom_call" | custom-call | tf_op jit(solution)/shard_map/pallas_call | solution.py:271
  33.2 0.0 copy-start
  33.2 5.9 all-to-all-start
  39.1 0.0 copy-done
  39.1 0.2 compare_reduce_fusion
  39.4 0.2 compare_reduce_fusion.1
  39.5 0.8 dynamic_slice.15
  40.4 0.7 reshape.164.keep
  41.0 0.2 fusion.1
  41.3 0.7 reshape.163.col_tab
  41.9 0.2 fusion.3
  42.1 0.1 broadcast_add_fusion
  42.2 0.7 reshape.162.row_tab
  42.9 0.6 pad_add_fusion.2.place
  43.5 718.9 %all-to-all-done = bf16[32,4,128,1024]{3,2,1,0:T(8,128)(2,1)} async-done(((bf16[32,4,128,1024]{3,2,1,0:T(8,128)(2,1)}), bf16[32,4,128,1024]{3,2,1,0:T(8,128)(2,1)}, u32[]{:S(2)}, u32[]{:S(2)}) %all-to-all-start) | async-done | bytes 33554464 | tf_op jit(solution)/shard_map/all_to_all | solution.py:288
  762.4 12.2 %shard_map.47.u_in = bf16[768,6144]{1,0:T(8,128)(2,1)} custom-call(s32[144]{0:T(256)} %reshape.162.row_tab, s32[288]{0:T(512)} %reshape.163.col_tab, bf16[8,4,4,128,1024]{4,3,2,1,0:T(8,128)(2,1)} %bitcast.5.t0.t1.refs_0_.refs_1_.refs_2_.refs_3_.refs_4_.refs_5_.refs_6_.refs_7_, ...), custom_call_target="tpu_custom_call" | custom-call | tf_op jit(solution)/shard_map/pallas_call | solution.py:302
  774.6 19.4 %shard_map.48.l_in = bf16[3072,768]{1,0:T(8,128)(2,1)} custom-call(s32[144]{0:T(256)} %reshape.162.row_tab, s32[288]{0:T(512)} %reshape.163.col_tab, s32[2]{0:T(128)} %pad_add_fusion.2.place, bf16[8,4,4,128,1024]{4,3,2,1,0:T(8,128)(2,1)} %bitcast.5.t0.t1.refs_0_.refs_1_.refs_2_.refs_3_.refs_4_.refs_5_.refs_6_.refs_7_, ...), custom_call_target="tpu_custom_call" | custom-call | tf_op jit(solution)/shard_map/pallas_call | solution.py:315
  794.0 150.9 %shard_map.49 = (bf16[768,6144]{1,0:T(8,128)(2,1)}, bf16[3072,768]{1,0:T(8,128)(2,1)}) custom-call(bf16[768,6144]{1,0:T(8,128)(2,1)} %shard_map.47.u_in, bf16[3072,768]{1,0:T(8,128)(2,1)} %shard_map.48.l_in), custom_call_target="tpu_custom_call", output_to_operand_aliasing={{0}: (0, {}), {1}: (1, {})} | custom-call | tf_op jit(solution)/shard_map/pallas_call | solution.py:229
  944.9 52.7 %shard_map.50 = bf16[3072,6144]{1,0:T(8,128)(2,1)} custom-call(s32[144]{0:T(256)} %reshape.162.row_tab, s32[288]{0:T(512)} %reshape.163.col_tab, s32[2]{0:T(128)} %pad_add_fusion.2.place, s32[1152]{0:T(1024)} %reshape.164.keep, bf16[8,4,4,128,1024]{4,3,2,1,0:T(8,128)(2,1)} %bitcast.5.t0.t1.refs_0_.refs_1_.refs_2_.refs_3_.refs_4_.refs_5_.refs_6_.refs_7_, ...), custom_call_target="tpu_custom_call" | custom-call | tf_op jit(solution)/shard_map/pallas_call | solution.py:330
  (8 shorter events, 0.1 us)
Async XLA Ops:
  33.2 5.9 copy-start
  33.2 729.2 %all-to-all-start = ((bf16[32,4,128,1024]{3,2,1,0:T(8,128)(2,1)}), bf16[32,4,128,1024]{3,2,1,0:T(8,128)(2,1)}, u32[]{:S(2)}, u32[]{:S(2)}) async-start(bf16[32,4,128,1024]{3,2,1,0:T(8,128)(2,1)} %bitcast.8), calls=%async_computation | async-start | bytes 67108864 | tf_op jit(solution)/shard_map/all_to_all | solution.py:288
